TPU v7x, 32 devices: a whole 2x2x4 slice. The times are simulated.
32 devices in a mesh: group: 2 (over x), module: 16 (over z, y, core).
Axes of the slice: x: 2, y: 2, z: 4, core: 2. Of those that a mesh axis runs over, the one named last changes fastest.
Arguments:
- query_grads: float32 [16, 32, 128, 128], P(None, None, 'module'), may hold values from -0.1875 to 0.1875
- train_grads: float32 [32, 128, 128, 128], P('module', 'group'), parts along dimension 1, may hold values from -0.1875 to 0.1875
- out_basis: float32 [32, 128, 128], P('module'), may hold values from -0.5 to 0.5
- in_basis: float32 [32, 128, 128], P('module'), may hold values from -0.5 to 0.5
- corrections: float32 [32, 128, 128], P('module'), may hold values from 0.01 to 10
- ranks: int32 [16], replicated, may hold values from 32 to 128
- slot_modules: int32 [32], replicated, may hold values from -1 to 15, as said below
Outputs:
- scores: float32 [32, 128], P(None, 'group'), parts along dimension 1
There are 2 independent parts, one for each index of `group`. A program takes and returns all parts, laid end to end along the dimension named above; an argument that names none is the same for every part. Nothing has to cross between parts.
Inputs may be any that keep to these rules, and one draw needn't show every extreme that they name: `slot_modules`: each module number 0 to 15 stands in exactly one entry; all other entries are -1. Owner i holds the 2 entries from i * 2 on, so an owner holds 0 to 2 modules, and some owner holds 2.
All inputs are finite; a program needn't handle non-finite values.
Results may differ from a plain program's by a relative error of at most 0.0003.
Values sent between devices are 32-bit elements; how exact they have to be, the bound alone decides.
A program may use at most 128 MiB of HBM per device.

v0:
```python
import jax
import jax.numpy as jnp
from jax import lax
from jax.sharding import PartitionSpec as P


def rotate(field, output_eigenbasis, inner_basis):
    inner = jnp.einsum("noi,ib->nob", field, inner_basis, precision=lax.Precision.HIGHEST)
    return jnp.einsum("oa,nob->nab", output_eigenbasis, inner, precision=lax.Precision.HIGHEST)


def blank_rotation(field, output_eigenbasis, inner_basis):
    return jnp.zeros(field.shape, jnp.float32)


def slot_weight(spectrum, keep_rank):
    damping = 0.1 * jnp.mean(spectrum)
    positions = lax.iota(jnp.int32, spectrum.shape[0])
    kept_mask = (positions[:, None] < keep_rank) & (positions[None, :] < keep_rank)
    return jnp.where(kept_mask, 1.0 / (spectrum + damping), jnp.zeros_like(spectrum))


def score_rotated(query_block, rotated_train, output_eigenbasis, inner_basis, spectrum, keep_rank):
    scaled = rotate(query_block, output_eigenbasis, inner_basis) * slot_weight(spectrum, keep_rank)
    return jnp.einsum("qab,eab->qe", scaled, rotated_train, precision=lax.Precision.HIGHEST)


def blank_scores(query_block, second_block, output_eigenbasis, inner_basis, spectrum, keep_rank):
    return jnp.zeros((query_block.shape[0], second_block.shape[0]), jnp.float32)


def body(query_grads, train_grads, out_basis, in_basis, corrections, ranks, slot_modules):
    slot_count = out_basis.shape[0]
    peer_count = lax.axis_size("module")
    own_index = lax.axis_index("module")
    owned_modules = lax.dynamic_slice_in_dim(slot_modules, own_index * slot_count, slot_count)
    query_count = query_grads.shape[1]
    example_count = train_grads.shape[1]
    rotated = []
    for number in range(slot_count):
        rotated.append(
            lax.cond(
                owned_modules[number] >= 0,
                rotate,
                blank_rotation,
                train_grads[number],
                out_basis[number],
                in_basis[number],
            )
        )
    safe_index = jnp.maximum(slot_modules, 0)
    populated_slots = slot_modules >= 0
    outgoing = jnp.where(populated_slots[:, None, None, None], query_grads[safe_index], 0.0)
    outgoing = outgoing.reshape((peer_count, slot_count) + outgoing.shape[1:])
    received = lax.all_to_all(outgoing, "module", split_axis=0, concat_axis=3, tiled=True)[0]
    running = jnp.zeros((query_count, example_count), jnp.float32)
    for number in range(slot_count):
        module = owned_modules[number]
        keep_rank = ranks[jnp.maximum(module, 0)]
        term = lax.cond(
            module >= 0,
            score_rotated,
            blank_scores,
            received[number],
            rotated[number],
            out_basis[number],
            in_basis[number],
            corrections[number],
            keep_rank,
        )
        running = running + term
    return lax.psum(running, "module")


def solution(mesh):
    return jax.shard_map(
        body,
        mesh=mesh,
        in_specs=(
            P(None, None, "module", None),
            P("module", "group", None, None),
            P("module", None, None),
            P("module", None, None),
            P("module", None, None),
            P(),
            P(),
        ),
        out_specs=P(None, "group"),
        check_vma=False,
    )
```

profile of v0, /device:TPU:0, one launch (start us, length us, event | category | flops | bytes accessed | tf_op | source)
XLA Modules:
  0.0 211.5 jit_solution(18283808478415897497)
XLA Ops:
  0.0 0.0 copy-start
  0.0 0.8 broadcast_maximum_fusion
  0.8 0.7 broadcast_compare_fusion
  1.5 0.1 broadcast_in_dim.24
  1.6 0.0 copy-done
  1.6 2.8 %gather_fusion = f32[32,32,8,128]{3,2,1,0:T(8,128)} fusion(f32[16,32,8,128]{3,2,1,0:T(8,128)S(1)} %copy-done, s32[1024]{0:T(1024)S(1)} %pad_clamp_fusion), kind=kCustom, calls=%fused_computation | custom fusion | bytes 8388736 | tf_op jit(solution)/shard_map/gather | solution.py:53
  4.4 4.8 %broadcast_select_fusion = f32[16,2,32,8,128]{4,3,2,1,0:T(8,128)} fusion(f32[16,2,32,8,128]{4,3,2,1,0:T(8,128)} %bitcast.80, pred[16,2]{1,0:T(8,128)(4,1)S(1)} %broadcast_in_dim.24), kind=kLoop, calls=%fused_computation.37 | loop fusion | flops 1048576 | bytes 8388640 | tf_op jit(solution)/shard_map/jit(_where)/select_n | solution.py:53
  9.1 7.6 %all-to-all-start = ((f32[16,2,32,8,128]{4,3,2,1,0:T(8,128)}), f32[16,2,32,8,128]{4,3,2,1,0:T(8,128)}, u32[]{:S(2)}, u32[]{:S(2)}) async-start(f32[16,2,32,8,128]{4,3,2,1,0:T(8,128)} %broadcast_select_fusion), calls=%async_computation | async-start | bytes 8388608 | tf_op jit(solution)/shard_map/all_to_all | solution.py:55
  16.7 0.0 copy-done.4
  16.7 0.1 dynamic_slice.11
  16.8 0.6 fusion.24
  18.7 0.0 copy-done.2
  18.7 0.0 copy-done.3
  18.8 2.5 %conditional.6 = (f32[64,128,128]{1,2,0:T(8,128)}) conditional(s32[]{:T(128)} %convert_element_type.9, () %tuple.34, (f32[2,64,128,128]{3,2,1,0:T(8,128)}, f32[128,128]{1,0:T(8,128)S(1)}, f32[128,128]{1,0:T(8,128)S(1)}) %tuple.35), branch_computations={%region_5.6_spmd, %region_6.0_spmd} | conditional | flops 3221225472 | bytes 16908296 | solution.py:42
  18.8 2.4 %broadcast.55 = f32[64,128,128]{1,2,0:T(8,128)} broadcast(f32[]{:T(128)} %constant.18.clone), dimensions={} | broadcast | bytes 4194308 | tf_op jit(solution)/shard_map/broadcast.4
  21.2 10.6 %conditional.4 = (f32[64,128,128]{1,2,0:T(8,128)}) conditional(s32[]{:T(128)} %convert_element_type.8, () %tuple.30, (f32[2,64,128,128]{3,2,1,0:T(8,128)}, f32[128,128]{1,0:T(8,128)S(1)}, f32[128,128]{1,0:T(8,128)S(1)}) %tuple.31), branch_computations={%region_0.0_spmd, %region_1.0_spmd} | conditional | flops 3221225472 | bytes 16908296 | solution.py:42
  21.2 5.7 %fusion = f32[64,128,128]{1,2,0:T(8,128)S(1)} fusion(f32[2,64,128,128]{3,2,1,0:T(8,128)} %get-tuple-element.77, f32[128,128]{1,0:T(8,128)S(1)} %get-tuple-element.78), kind=kOutput, calls=%fused_computation.1 | convolution fusion | flops 1610612736 | bytes 8454144 | tf_op jit(solution)/shard_map/cond/branch_1_fun/noi,ib->nob/dot_general | solution.py:8
  26.9 4.9 %convolution_bitcast_fusion = f32[64,128,128]{1,2,0:T(8,128)} fusion(f32[64,128,128]{1,2,0:T(8,128)S(1)} %fusion, f32[128,128]{1,0:T(8,128)S(1)} %get-tuple-element.79), kind=kOutput, calls=%fused_computation.4 | convolution fusion | flops 1610612736 | bytes 8454144 | tf_op jit(solution)/shard_map/cond/branch_1_fun/oa,nob->nab/dot_general | solution.py:9
  31.8 62.6 %all-to-all-done = f32[16,2,32,8,128]{4,3,2,1,0:T(8,128)} async-done(((f32[16,2,32,8,128]{4,3,2,1,0:T(8,128)}), f32[16,2,32,8,128]{4,3,2,1,0:T(8,128)}, u32[]{:S(2)}, u32[]{:S(2)}) %all-to-all-start) | async-done | bytes 4194336 | tf_op jit(solution)/shard_map/all_to_all | solution.py:55
  94.4 0.0 copy-done.1
  94.4 0.2 conditional.7
  94.6 26.6 %conditional.5 = (f32[32,64]{1,0:T(8,128)S(1)}) conditional(s32[]{:T(128)} %convert_element_type.8, () %tuple.29, (f32[1,2,32,16,8,128]{5,4,2,1,3,0:T(8,128)}, f32[128,128]{1,0:T(8,128)S(1)}, f32[128,128]{1,0:T(8,128)S(1)}, s32[]{:T(128)}, s32[16]{0:T(128)S(1)}, /*index=5*/f32[2,128,128]{2,1,0:T(8,128)S(1)}, f32[64,128,128]{1,2,0:T(8,128)}) %tuple.57), branch_computations={%region_2.0_spmd, %region_3.5_spmd} | conditional | flops 2013872256 | bytes 27665592 | solution.py:60
  94.8 0.6 slice_reduce_fusion
  96.8 0.6 dynamic_slice.8
  97.4 0.6 iota_compare_fusion
  98.0 0.1 bitcast_select_fusion
  98.1 3.5 %fusion.5 = f32[32,128,128]{2,1,0:T(8,128)S(1)} fusion(f32[128,128]{1,0:T(8,128)S(1)} %get-tuple-element.81, f32[1,2,32,16,8,128]{5,4,2,1,3,0:T(8,128)} %get-tuple-element.111), kind=kOutput, calls=%fused_computation.8 | convolution fusion | flops 805306368 | bytes 4259840 | tf_op jit(solution)/shard_map/cond/branch_1_fun/noi,ib->nob/dot_general | solution.py:8
  101.6 4.9 %fusion.9 = f32[32,128,128]{2,1,0:T(8,128)} fusion(f32[32,128,128]{2,1,0:T(8,128)S(1)} %fusion.5, f32[128,128]{1,0:T(8,128)S(1)} %get-tuple-element.82), kind=kOutput, calls=%fused_computation.14 | convolution fusion | flops 805306368 | bytes 4259840 | tf_op jit(solution)/shard_map/cond/branch_1_fun/oa,nob->nab/dot_general | solution.py:9
  106.5 3.1 %copy.15 = f32[32,128,128]{1,0,2:T(8,128)} copy(f32[32,128,128]{2,1,0:T(8,128)} %fusion.9) | data formatting | bytes 4194304 | tf_op jit(solution)/shard_map/cond/branch_1_fun/oa,nob->nab/dot_general | solution.py:9
  109.5 5.4 %copy.12 = f32[64,128,128]{2,0,1:T(8,128)} copy(f32[64,128,128]{1,2,0:T(8,128)} %get-tuple-element.117) | data formatting | bytes 8388608 | tf_op jit(solution)/shard_map
  114.9 6.2 %fusion.7 = f32[32,64]{1,0:T(8,128)S(1)} fusion(f32[64,128,128]{2,0,1:T(8,128)} %copy.12, f32[32,128,128]{1,0,2:T(8,128)} %copy.15, f32[128,128]{1,0:T(8,128)S(1)} %bitcast_select_fusion), kind=kOutput, calls=%fused_computation.11 | convolution fusion | flops 403177472 | bytes 6365184 | tf_op jit(solution)/shard_map/cond/branch_1_fun/qab,eab->qe/dot_general | solution.py:25
  121.2 90.4 %psum.7 = f32[32,64]{1,0:T(8,128)} all-reduce(f32[32,64]{1,0:T(8,128)S(1)} %add.27), channel_id=1, replica_groups=mesh['group'=2,'module'=16] {'module'}, use_global_device_ids=true, to_apply=%region_10.11 | all-reduce | flops 2048 | bytes 16384 | tf_op jit(solution)/shard_map/psum | solution.py:72
  (10 shorter events, 0.0 us)
Async XLA Ops:
  0.0 1.6 copy-start
  9.1 7.6 %copy-start.4 = (s32[32]{0:T(128)S(1)}, s32[32]{0:T(128)}, u32[]{:S(2)}) copy-start(s32[32]{0:T(128)} %param.21) | copy-start | bytes 388
  9.1 9.6 %copy-start.2 = (f32[2,128,128]{2,1,0:T(8,128)S(1)}, f32[2,128,128]{2,1,0:T(8,128)}, u32[]{:S(2)}) copy-start(f32[2,128,128]{2,1,0:T(8,128)} %param.17) | copy-start | bytes 393220
  9.1 9.6 %copy-start.3 = (f32[2,128,128]{2,1,0:T(8,128)S(1)}, f32[2,128,128]{2,1,0:T(8,128)}, u32[]{:S(2)}) copy-start(f32[2,128,128]{2,1,0:T(8,128)} %param.18) | copy-start | bytes 393220
  9.1 85.3 %all-to-all-start = ((f32[16,2,32,8,128]{4,3,2,1,0:T(8,128)}), f32[16,2,32,8,128]{4,3,2,1,0:T(8,128)}, u32[]{:S(2)}, u32[]{:S(2)}) async-start(f32[16,2,32,8,128]{4,3,2,1,0:T(8,128)} %broadcast_select_fusion), calls=%async_computation | async-start | bytes 8388608 | tf_op jit(solution)/shard_map/all_to_all | solution.py:55
  21.2 73.2 %copy-start.1 = (f32[2,128,128]{2,1,0:T(8,128)S(1)}, f32[2,128,128]{2,1,0:T(8,128)}, u32[]{:S(2)}) copy-start(f32[2,128,128]{2,1,0:T(8,128)} %param.19) | copy-start | bytes 393220
  21.2 73.2 %copy-start.5 = (s32[16]{0:T(128)S(1)}, s32[16]{0:T(128)}, u32[]{:S(2)}) copy-start(s32[16]{0:T(128)} %param.20) | copy-start | bytes 196
where the time goes:
time: 211 us; the launch traced here: 212 us
  blocking collectives  90.4 us (43%)
  waiting for transfers between devices  62.6 us (30%)
  matrix products  25.1 us (12%)
  local copies, waits for them, and re-layouts  15.1 us (7%)
  other arithmetic  7.58 us (4%)
  starting transfers between devices  7.57 us (4%)
    psum x1, blocking collectives, body(): return lax.psum(running, 'module')  90.4 us
    all_to_all x1, waiting for transfers between devices, body(): lax.all_to_all(outgoing, 'module', split_axis=0, concat_axis=3, tiled=True)  62.6 us
    dot_general x2, matrix products, rotate(): jnp.einsum('oa,nob->nab', output_eigenbasis, inner, precision=lax.Precisi...  9.78 us
    dot_general x2, matrix products, rotate(): jnp.einsum('noi,ib->nob', field, inner_basis, precision=lax.Precision.HIG...  9.11 us
    another operation x3, local copies, waits for them, and re-layouts  7.84 us
    all_to_all x1, starting transfers between devices, body(): lax.all_to_all(outgoing, 'module', split_axis=0, concat_axis=3, tiled=True)  7.57 us
    dot_general x1, matrix products, score_rotated(): jnp.einsum('qab,eab->qe', scaled, rotated_train, precision=lax.Precision....  6.22 us
    select_n x1, other arithmetic, body(): jnp.where(populated_slots[:, None, None, None], query_grads[safe_index],...  4.75 us
  transfers between devices with their start and end apart: 1, of which 1 were waited for; matrix products, arithmetic and copies ran while one was open for 6% of the time, Pallas kernels for 0%

commit v1 on v0

v1 whole, which is shorter than its diff:
```python
import functools

import jax
import jax.numpy as jnp
from jax import lax
from jax.experimental import pallas as pl
from jax.experimental.pallas import tpu as pltpu
from jax.sharding import PartitionSpec as P

MESH = pl.DeviceIdType.MESH
F32 = jnp.float32
BF16 = jnp.bfloat16
PAIRS = 4


def split(x):
    high = x.astype(BF16)
    low = (x - high.astype(F32)).astype(BF16)
    return high, low


def halves_beside(x):
    high, low = split(x)
    return jnp.concatenate([high, low], axis=1)


def halves_below(x):
    high, low = split(x)
    return jnp.concatenate([high, low], axis=0)


def kernel(
    n, groups,
    slots_ref, ranks_ref, query_ref, train_ref, out_basis_ref, in_basis_ref, spectrum_ref,
    scores_ref,
    outgoing, received, train, left, right, weights, total, part, parts,
    train_sem, send_sem, recv_sem, pass_sem, passed_sem, sum_send_sem, sum_recv_sem,
):
    me = lax.axis_index("module")
    group = lax.axis_index("group")
    slots, dim = out_basis_ref.shape[0], out_basis_ref.shape[1]
    share, rows = received.shape[3], received.shape[4]
    examples = train_ref.shape[1] // dim
    queries = share * groups

    def peer(index):
        return (group, index)

    def group_peer(step):
        return (lax.rem(group + step, groups), me)

    load_train = [
        pltpu.make_async_copy(train_ref.at[k], train.at[k], train_sem.at[k]) for k in range(slots)
    ]
    for copy in load_train:
        copy.start()

    barrier = pltpu.get_barrier_semaphore()

    def greet(step, carry):
        pl.semaphore_signal(
            barrier, inc=1, device_id=peer(lax.rem(me + step, n)), device_id_type=MESH
        )
        return carry

    lax.fori_loop(1, n, greet, 0)
    for step in range(1, groups):
        pl.semaphore_signal(barrier, inc=1, device_id=group_peer(step), device_id_type=MESH)

    def offset(turn):
        return lax.rem(4 - lax.rem(turn, 4), 4) * (n // 4) + turn // 4

    def fill(turn, carry):
        target = lax.rem(me + offset(turn), n)
        for k in range(slots):
            module = jnp.maximum(slots_ref[target * slots + k], 0)
            outgoing[turn, k] = query_ref[module, pl.ds(group * share, share)]
        return carry

    lax.fori_loop(1, n, fill, 0)
    for k in range(slots):
        module = jnp.maximum(slots_ref[me * slots + k], 0)
        for g in range(groups):
            received[g, me, k] = query_ref[module, pl.ds(g * share, share)]

    pl.semaphore_wait(barrier, n - 1 + groups - 1)

    def message(turn, k):
        return pltpu.make_async_remote_copy(
            src_ref=outgoing.at[turn, k],
            dst_ref=received.at[group, me, k],
            send_sem=send_sem.at[turn, k],
            recv_sem=recv_sem.at[turn, k],
            device_id=peer(lax.rem(me + offset(turn), n)),
            device_id_type=MESH,
        )

    def send(turn, carry):
        for k in range(slots):
            message(turn, k).start()
        return carry

    lax.fori_loop(1, n, send, 0)

    def source(turn):
        return lax.rem(me + n - offset(turn), n)

    def arrival(turn, k):
        block = received.at[group, source(turn), k]
        return pltpu.make_async_remote_copy(
            src_ref=block,
            dst_ref=block,
            send_sem=send_sem.at[turn, k],
            recv_sem=recv_sem.at[turn, k],
            device_id=peer(source(turn)),
            device_id_type=MESH,
        )

    def hand_on(step, turn, k):
        block = received.at[group, source(turn), k]
        return pltpu.make_async_remote_copy(
            src_ref=block,
            dst_ref=block,
            send_sem=pass_sem.at[step, turn, k],
            recv_sem=passed_sem.at[step, turn, k],
            device_id=group_peer(step),
            device_id_type=MESH,
        )

    def handed(step, turn, k):
        giver = lax.rem(group + groups - step, groups)
        block = received.at[giver, source(turn), k]
        return pltpu.make_async_remote_copy(
            src_ref=block,
            dst_ref=block,
            send_sem=pass_sem.at[step, turn, k],
            recv_sem=passed_sem.at[step, turn, k],
            device_id=group_peer(step),
            device_id_type=MESH,
        )

    def turn_of(number):
        return number // slots + 1, lax.rem(number, slots)

    def forward(number):
        turn, k = turn_of(number)
        arrival(turn, k).wait_recv()
        for step in range(1, groups):
            hand_on(step, turn, k).start()

    for k in range(slots):
        u, v = out_basis_ref[k], in_basis_ref[k]
        for at, matrix in ((0, u.T), (1, u)):
            stacked = halves_below(matrix)
            left[k, at] = jnp.concatenate([stacked, stacked], axis=1)
        for at, matrix in ((0, v), (1, v.T)):
            beside = halves_beside(matrix)
            right[k, at] = jnp.concatenate([beside, beside], axis=0)
        module = slots_ref[me * slots + k]
        keep = jnp.where(module >= 0, ranks_ref[jnp.maximum(module, 0)], 0)
        spectrum = spectrum_ref[k]
        damping = 0.1 * jnp.mean(spectrum)
        kept = (lax.broadcasted_iota(jnp.int32, (dim, dim), 0) < keep) & (
            lax.broadcasted_iota(jnp.int32, (dim, dim), 1) < keep
        )
        weight = jnp.where(kept, 1.0 / (spectrum + damping), jnp.zeros_like(spectrum))
        weights[k] = jnp.concatenate([weight, weight], axis=1)

    def times_right(x, factor):
        product = jnp.dot(halves_beside(x), factor, preferred_element_type=F32)
        return product[:, :dim] + product[:, dim:]

    def times_left(factor, x):
        product = jnp.dot(factor, halves_below(x), preferred_element_type=F32)
        return product[:dim] + product[dim:]

    def side_by_side(x):
        return jnp.concatenate([x[:dim], x[dim:]], axis=1)

    def one_below_other(x):
        return jnp.concatenate([x[:, :dim], x[:, dim:]], axis=0)

    steps = examples // (2 * PAIRS)
    count = (n - 1) * slots
    early = min(count, steps * slots)

    for k in range(slots):
        load_train[k].wait()

        def rotate(step, carry, k=k):
            for pair in range(PAIRS):
                place = pl.ds((step * PAIRS + pair) * 2 * dim, 2 * dim)
                x = times_right(train[k, place], right[k, 0])
                x = times_left(left[k, 0], side_by_side(x)) * weights[k]
                x = times_right(one_below_other(x), right[k, 1])
                x = times_left(left[k, 1], side_by_side(x))
                train[k, place] = one_below_other(x)
            if early == steps * slots:
                forward(k * steps + step)
            return carry

        lax.fori_loop(0, steps, rotate, 0)

    if early != steps * slots:
        early = 0
    total[...] = jnp.zeros_like(total)

    def score(origin, k):
        added = jnp.zeros_like(total)
        for row in range(0, rows, 2):
            asked, given = [], []
            for r in (row, row + 1):
                block = jnp.concatenate(
                    [received[g, origin, k, :, r, :] for g in range(groups)], axis=0
                )
                asked.append(halves_below(block))
                taken = train[k, pl.ds(origin * rows + r, examples, stride=dim), :]
                given.append(halves_below(taken))
            added += lax.dot_general(
                jnp.concatenate(asked, axis=1),
                jnp.concatenate(given, axis=1),
                (((1,), (1,)), ((), ())),
                preferred_element_type=F32,
            )
        total[...] += added

    def use(number):
        turn, k = turn_of(number)
        for step in range(1, groups):
            handed(step, turn, k).wait_recv()
        score(source(turn), k)

    for k in range(slots):
        score(me, k)

    late = count - early
    twice = max(0, min(late, early - 2, count // 2))

    def both(i, carry):
        forward(early + i)
        use(2 * i)
        use(2 * i + 1)
        return carry

    lax.fori_loop(0, twice, both, 0)
    lag = early - twice
    if lag == 0 and late > twice:
        lag = 2
        for i in range(lag):
            forward(early + twice + i)
        begun = early + twice + lag
    else:
        begun = early + twice

    def single(number, carry):
        forward(number)
        use(number - lag)
        return carry

    lax.fori_loop(begun, count, single, 0)
    done = max(2 * twice, count - lag) if begun < count else 2 * twice

    def rest(number, carry):
        use(number)
        return carry

    lax.fori_loop(done, count, rest, 0)

    summed = total[...]
    summed = summed[:queries] + summed[queries:]
    summed = summed[:, :examples] + summed[:, examples:]
    half = queries // 2
    part[...] = jnp.concatenate([summed[:half], summed[half:]], axis=1)

    def partial(step):
        return pltpu.make_async_remote_copy(
            src_ref=part,
            dst_ref=parts.at[step],
            send_sem=sum_send_sem.at[step],
            recv_sem=sum_recv_sem.at[step],
            device_id=peer(lax.rem(me + step, n)),
            device_id_type=MESH,
        )

    def share_partial(step, carry):
        partial(step).start()
        return carry

    lax.fori_loop(1, n, share_partial, 0)
    parts[0] = part[...]

    def sent(turn, carry):
        for k in range(slots):
            message(turn, k).wait_send()
            for step in range(1, groups):
                hand_on(step, turn, k).wait_send()
        return carry

    lax.fori_loop(1, n, sent, 0)

    def arrived(step, carry):
        partial(step).wait_recv()
        return carry

    lax.fori_loop(1, n, arrived, 0)

    def add(owner, running):
        return running + parts[lax.rem(me + n - owner, n)]

    final = lax.fori_loop(0, n, add, jnp.zeros_like(part))
    scores_ref[...] = jnp.concatenate([final[:, :examples], final[:, examples:]], axis=0)

    def drained(step, carry):
        partial(step).wait_send()
        return carry

    lax.fori_loop(1, n, drained, 0)


def body(n, groups, query_grads, train_grads, out_basis, in_basis, corrections, ranks, slot_modules):
    modules, queries, rows, dim = query_grads.shape
    slots, examples = train_grads.shape[:2]
    share = queries // groups
    vmem = pl.BlockSpec(memory_space=pltpu.VMEM)
    smem = pl.BlockSpec(memory_space=pltpu.SMEM)
    return pl.pallas_call(
        functools.partial(kernel, n, groups),
        out_shape=jax.ShapeDtypeStruct((queries, examples), F32),
        in_specs=[smem, smem, vmem, pl.BlockSpec(memory_space=pl.ANY), vmem, vmem, vmem],
        out_specs=vmem,
        scratch_shapes=[
            pltpu.VMEM((n, slots, share, rows, dim), F32),
            pltpu.VMEM((groups, n, slots, share, rows, dim), F32),
            pltpu.VMEM((slots, examples * dim, dim), F32),
            pltpu.VMEM((slots, 2, 2 * dim, 2 * dim), BF16),
            pltpu.VMEM((slots, 2, 2 * dim, 2 * dim), BF16),
            pltpu.VMEM((slots, dim, 2 * dim), F32),
            pltpu.VMEM((2 * queries, 2 * examples), F32),
            pltpu.VMEM((queries // 2, 2 * examples), F32),
            pltpu.VMEM((n, queries // 2, 2 * examples), F32),
            pltpu.SemaphoreType.DMA((slots,)),
            pltpu.SemaphoreType.DMA((n, slots)),
            pltpu.SemaphoreType.DMA((n, slots)),
            pltpu.SemaphoreType.DMA((groups, n, slots)),
            pltpu.SemaphoreType.DMA((groups, n, slots)),
            pltpu.SemaphoreType.DMA((n,)),
            pltpu.SemaphoreType.DMA((n,)),
        ],
        compiler_params=pltpu.CompilerParams(
            collective_id=0, has_side_effects=True, vmem_limit_bytes=48 * 1024 * 1024
        ),
    )(
        slot_modules, ranks, query_grads, train_grads.reshape(slots, examples * dim, dim),
        out_basis, in_basis, corrections,
    )


def solution(mesh):
    return jax.shard_map(
        functools.partial(body, mesh.shape["module"], mesh.shape["group"]),
        mesh=mesh,
        in_specs=(
            P(None, None, "module", None),
            P("module", "group", None, None),
            P("module", None, None),
            P("module", None, None),
            P("module", None, None),
            P(),
            P(),
        ),
        out_specs=P(None, "group"),
        check_vma=False,
    )
```

time: 211 us -> 86.2 us (0.41)
  blocking collectives: 90.4 us -> 0 us
  Pallas kernels: 0 us -> 79.7 us
  waiting for transfers between devices: 62.6 us -> 0 us
  matrix products: 25.1 us -> 0 us
  local copies, waits for them, and re-layouts: 15.1 us -> 6.22 us
  other arithmetic: 7.58 us -> 0 us
  starting transfers between devices: 7.57 us -> 0 us
    psum x1 -> x0, blocking collectives: 90.4 us -> none  [body(): return lax.psum(running, 'module')]
    pallas_call x0 -> x1, Pallas kernels: none -> 79.7 us  [body(): pl.pallas_call(functools.partial(kernel, n, groups), out_shape=jax.ShapeD...]
    all_to_all x1 -> x0, waiting for transfers between devices: 62.6 us -> none  [body(): lax.all_to_all(outgoing, 'module', split_axis=0, concat_axis=3, tiled=True)]
    dot_general x5 -> x0, matrix products: 25.1 us -> none  [the longest x2 9.78 us: rotate(): jnp.einsum('oa,nob->nab', output_eigenbasis, inner, precision=lax.Precisi...]
    another operation x3 -> x0, local copies, waits for them, and re-layouts: 7.84 us -> none
    all_to_all x1 -> x0, starting transfers between devices: 7.57 us -> none  [body(): lax.all_to_all(outgoing, 'module', split_axis=0, concat_axis=3, tiled=True)]
    unnamed x12 -> x13, local copies, waits for them, and re-layouts: 0.06 us -> 6.22 us
    select_n x2 -> x0, other arithmetic: 4.84 us -> none  [the longest x1 4.75 us: body(): jnp.where(populated_slots[:, None, None, None], query_grads[safe_index],...]
  transfers between devices with their start and end apart: 1 -> 0, of which waited for: 1 -> 0; matrix products, arithmetic and copies ran while one was open for 6% -> 0% of each run, Pallas kernels for 0% -> 0%
where the time goes in v1:
time: 86.2 us; the launch traced here: 86 us
  Pallas kernels  79.7 us (92%)
  local copies, waits for them, and re-layouts  6.22 us (7%)
    pallas_call x1, Pallas kernels, body(): pl.pallas_call(functools.partial(kernel, n, groups), out_shape=jax.ShapeD...  79.7 us
    unnamed x13, local copies, waits for them, and re-layouts  6.22 us

profile of v1, /device:TPU:0, one launch (start us, length us, event | category | flops | bytes accessed | tf_op | source)
XLA Modules:
  0.0 86.0 jit_solution(11341013035267321491)
XLA Ops:
  0.0 0.0 copy-start
  0.0 1.6 %copy-done = f32[16,32,8,128]{3,2,1,0:T(8,128)S(1)} copy-done((f32[16,32,8,128]{3,2,1,0:T(8,128)S(1)}, f32[16,32,8,128]{3,2,1,0:T(8,128)}, u32[]{:S(2)}) %copy-start) | copy-done | bytes 2097176
  1.6 0.0 copy-start.1
  1.6 0.9 %copy-done.1 = f32[2,128,128]{2,1,0:T(8,128)S(1)} copy-done((f32[2,128,128]{2,1,0:T(8,128)S(1)}, f32[2,128,128]{2,1,0:T(8,128)}, u32[]{:S(2)}) %copy-start.1) | copy-done | bytes 131096
  2.5 0.0 copy-start.2
  2.5 0.9 %copy-done.2 = f32[2,128,128]{2,1,0:T(8,128)S(1)} copy-done((f32[2,128,128]{2,1,0:T(8,128)S(1)}, f32[2,128,128]{2,1,0:T(8,128)}, u32[]{:S(2)}) %copy-start.2) | copy-done | bytes 131096
  3.4 0.0 copy-start.3
  3.4 0.9 %copy-done.3 = f32[2,128,128]{2,1,0:T(8,128)S(1)} copy-done((f32[2,128,128]{2,1,0:T(8,128)S(1)}, f32[2,128,128]{2,1,0:T(8,128)}, u32[]{:S(2)}) %copy-start.3) | copy-done | bytes 131096
  4.3 0.0 copy-start.4
  4.3 0.7 copy-done.4
  5.0 0.0 copy-start.5
  5.0 0.7 copy-done.5
  5.6 79.7 %shard_map.73 = f32[32,64]{1,0:T(8,128)S(1)} custom-call(s32[32]{0:T(128)S(1)} %copy-done.4, s32[16]{0:T(128)S(1)} %copy-done.5, f32[16,32,8,128]{3,2,1,0:T(8,128)S(1)} %copy-done, f32[2,8192,128]{2,1,0:T(8,128)} %bitcast.1, f32[2,128,128]{2,1,0:T(8,128)S(1)} %copy-done.1, f32[2,128,128]{2,1,0:T(8,128)S(1)} %copy-done.2, f32[2,128,128]{2,1,0:T(8,128)S(1)} %copy-done.3), custom_call_target="tpu_custom_call" | custom-call | tf_op jit(solution)/shard_map/pallas_call | solution.py:326
  85.4 0.6 copy.9
Async XLA Ops:
  0.0 1.6 %copy-start = (f32[16,32,8,128]{3,2,1,0:T(8,128)S(1)}, f32[16,32,8,128]{3,2,1,0:T(8,128)}, u32[]{:S(2)}) copy-start(f32[16,32,8,128]{3,2,1,0:T(8,128)} %query_ref.1) | copy-start | bytes 6291460
  1.6 0.9 %copy-start.1 = (f32[2,128,128]{2,1,0:T(8,128)S(1)}, f32[2,128,128]{2,1,0:T(8,128)}, u32[]{:S(2)}) copy-start(f32[2,128,128]{2,1,0:T(8,128)} %out_basis_ref.1) | copy-start | bytes 393220
  2.5 0.9 %copy-start.2 = (f32[2,128,128]{2,1,0:T(8,128)S(1)}, f32[2,128,128]{2,1,0:T(8,128)}, u32[]{:S(2)}) copy-start(f32[2,128,128]{2,1,0:T(8,128)} %in_basis_ref.1) | copy-start | bytes 393220
  3.4 0.9 %copy-start.3 = (f32[2,128,128]{2,1,0:T(8,128)S(1)}, f32[2,128,128]{2,1,0:T(8,128)}, u32[]{:S(2)}) copy-start(f32[2,128,128]{2,1,0:T(8,128)} %spectrum_ref.1) | copy-start | bytes 393220
  4.3 0.7 copy-start.4
  5.0 0.7 copy-start.5

commit v2 on v1

--- a/solution.py
+++ b/solution.py
@@ -31,15 +31,17 @@
 
 def kernel(
     n, groups,
-    slots_ref, ranks_ref, query_ref, train_ref, out_basis_ref, in_basis_ref, spectrum_ref,
+    slots_hbm, ranks_hbm, query_hbm, train_ref, out_basis_hbm, in_basis_hbm, spectrum_hbm,
     scores_ref,
-    outgoing, received, train, left, right, weights, total, part, parts,
-    train_sem, send_sem, recv_sem, pass_sem, passed_sem, sum_send_sem, sum_recv_sem,
+    slots_ref, ranks_ref, query_ref, out_basis_ref, in_basis_ref, spectrum_ref,
+    outgoing, direct, received, train, left, right, weights, total, part, parts,
+    load_sem, train_sem, send_sem, recv_sem, direct_send_sem, direct_recv_sem, pass_sem, passed_sem, sum_send_sem, sum_recv_sem,
 ):
     me = lax.axis_index("module")
     group = lax.axis_index("group")
     slots, dim = out_basis_ref.shape[0], out_basis_ref.shape[1]
     share, rows = received.shape[3], received.shape[4]
+    part_size = n // 2
     examples = train_ref.shape[1] // dim
     queries = share * groups
 
@@ -48,6 +50,34 @@
 
     def group_peer(step):
         return (lax.rem(group + step, groups), me)
+
+    loads = [
+        pltpu.make_async_copy(source_ref, target_ref, load_sem.at[at])
+        for at, (source_ref, target_ref) in enumerate(
+            (
+                (slots_hbm, slots_ref),
+                (query_hbm, query_ref),
+                (ranks_hbm, ranks_ref),
+                (out_basis_hbm, out_basis_ref),
+                (in_basis_hbm, in_basis_ref),
+                (spectrum_hbm, spectrum_ref),
+            )
+        )
+    ]
+    for copy in loads:
+        copy.start()
+
+    barrier = pltpu.get_barrier_semaphore()
+
+    def greet(step, carry):
+        pl.semaphore_signal(
+            barrier, inc=1, device_id=peer(lax.rem(me + step, n)), device_id_type=MESH
+        )
+        return carry
+
+    lax.fori_loop(1, n, greet, 0)
+    for step in range(1, groups):
+        pl.semaphore_signal(barrier, inc=1, device_id=group_peer(step), device_id_type=MESH)
 
     load_train = [
         pltpu.make_async_copy(train_ref.at[k], train.at[k], train_sem.at[k]) for k in range(slots)
@@ -55,43 +85,52 @@
     for copy in load_train:
         copy.start()
 
-    barrier = pltpu.get_barrier_semaphore()
-
-    def greet(step, carry):
-        pl.semaphore_signal(
-            barrier, inc=1, device_id=peer(lax.rem(me + step, n)), device_id_type=MESH
-        )
-        return carry
-
-    lax.fori_loop(1, n, greet, 0)
-    for step in range(1, groups):
-        pl.semaphore_signal(barrier, inc=1, device_id=group_peer(step), device_id_type=MESH)
-
-    def offset(turn):
-        return lax.rem(4 - lax.rem(turn, 4), 4) * (n // 4) + turn // 4
+    mine = me // part_size
+    place = lax.rem(me, part_size)
+
+    def across(turn):
+        return (1 - mine) * part_size + lax.rem(place + turn, part_size)
+
+    def within(turn):
+        return mine * part_size + lax.rem(place + turn, part_size)
+
+    def source(turn):
+        return (1 - mine) * part_size + lax.rem(place + part_size - turn, part_size)
+
+    def near_source(turn):
+        return mine * part_size + lax.rem(place + part_size - turn, part_size)
+
+    def wanted(target, k):
+        return jnp.maximum(slots_ref[target * slots + k], 0)
+
+    loads[0].wait()
+    loads[1].wait()
 
     def fill(turn, carry):
-        target = lax.rem(me + offset(turn), n)
         for k in range(slots):
-            module = jnp.maximum(slots_ref[target * slots + k], 0)
-            outgoing[turn, k] = query_ref[module, pl.ds(group * share, share)]
-        return carry
-
-    lax.fori_loop(1, n, fill, 0)
-    for k in range(slots):
-        module = jnp.maximum(slots_ref[me * slots + k], 0)
-        for g in range(groups):
-            received[g, me, k] = query_ref[module, pl.ds(g * share, share)]
-
+            outgoing[turn, k] = query_ref[wanted(across(turn), k), pl.ds(group * share, share)]
+        return carry
+
+    lax.fori_loop(0, part_size, fill, 0)
     pl.semaphore_wait(barrier, n - 1 + groups - 1)
 
     def message(turn, k):
         return pltpu.make_async_remote_copy(
             src_ref=outgoing.at[turn, k],
-            dst_ref=received.at[group, me, k],
+            dst_ref=received.at[me, k, group],
             send_sem=send_sem.at[turn, k],
             recv_sem=recv_sem.at[turn, k],
-            device_id=peer(lax.rem(me + offset(turn), n)),
+            device_id=peer(across(turn)),
+            device_id_type=MESH,
+        )
+
+    def near_message(turn, k):
+        return pltpu.make_async_remote_copy(
+            src_ref=direct.at[turn, k],
+            dst_ref=received.at[me, k],
+            send_sem=direct_send_sem.at[turn, k],
+            recv_sem=direct_recv_sem.at[turn, k],
+            device_id=peer(within(turn)),
             device_id_type=MESH,
         )
 
@@ -100,13 +139,22 @@
             message(turn, k).start()
         return carry
 
-    lax.fori_loop(1, n, send, 0)
-
-    def source(turn):
-        return lax.rem(me + n - offset(turn), n)
+    lax.fori_loop(0, part_size, send, 0)
+
+    def send_near(turn, carry):
+        for k in range(slots):
+            for g in range(groups):
+                direct[turn, k, g] = query_ref[wanted(within(turn), k), pl.ds(g * share, share)]
+            near_message(turn, k).start()
+        return carry
+
+    lax.fori_loop(1, part_size, send_near, 0)
+    for k in range(slots):
+        for g in range(groups):
+            received[me, k, g] = query_ref[wanted(me, k), pl.ds(g * share, share)]
 
     def arrival(turn, k):
-        block = received.at[group, source(turn), k]
+        block = received.at[source(turn), k, group]
         return pltpu.make_async_remote_copy(
             src_ref=block,
             dst_ref=block,
@@ -116,8 +164,19 @@
             device_id_type=MESH,
         )
 
+    def near_arrival(turn, k):
+        block = received.at[near_source(turn), k]
+        return pltpu.make_async_remote_copy(
+            src_ref=block,
+            dst_ref=block,
+            send_sem=direct_send_sem.at[turn, k],
+            recv_sem=direct_recv_sem.at[turn, k],
+            device_id=peer(near_source(turn)),
+            device_id_type=MESH,
+        )
+
     def hand_on(step, turn, k):
-        block = received.at[group, source(turn), k]
+        block = received.at[source(turn), k, group]
         return pltpu.make_async_remote_copy(
             src_ref=block,
             dst_ref=block,
@@ -129,7 +188,7 @@
 
     def handed(step, turn, k):
         giver = lax.rem(group + groups - step, groups)
-        block = received.at[giver, source(turn), k]
+        block = received.at[source(turn), k, giver]
         return pltpu.make_async_remote_copy(
             src_ref=block,
             dst_ref=block,
@@ -140,13 +199,16 @@
         )
 
     def turn_of(number):
-        return number // slots + 1, lax.rem(number, slots)
+        return number // slots, lax.rem(number, slots)
 
     def forward(number):
         turn, k = turn_of(number)
         arrival(turn, k).wait_recv()
         for step in range(1, groups):
             hand_on(step, turn, k).start()
+
+    for copy in loads[2:]:
+        copy.wait()
 
     for k in range(slots):
         u, v = out_basis_ref[k], in_basis_ref[k]
@@ -181,8 +243,8 @@
         return jnp.concatenate([x[:, :dim], x[:, dim:]], axis=0)
 
     steps = examples // (2 * PAIRS)
-    count = (n - 1) * slots
-    early = min(count, steps * slots)
+    count = part_size * slots
+    early = steps // 2 + (slots - 1) * steps
 
     for k in range(slots):
         load_train[k].wait()
@@ -195,14 +257,14 @@
                 x = times_right(one_below_other(x), right[k, 1])
                 x = times_left(left[k, 1], side_by_side(x))
                 train[k, place] = one_below_other(x)
-            if early == steps * slots:
-                forward(k * steps + step)
+            if k == 0:
+                pl.when(lax.rem(step, 2) == 1)(lambda: forward(step // 2))
+            else:
+                forward(steps // 2 + (k - 1) * steps + step)
             return carry
 
         lax.fori_loop(0, steps, rotate, 0)
 
-    if early != steps * slots:
-        early = 0
     total[...] = jnp.zeros_like(total)
 
     def score(origin, k):
@@ -211,7 +273,7 @@
             asked, given = [], []
             for r in (row, row + 1):
                 block = jnp.concatenate(
-                    [received[g, origin, k, :, r, :] for g in range(groups)], axis=0
+                    [received[origin, k, g, :, r, :] for g in range(groups)], axis=0
                 )
                 asked.append(halves_below(block))
                 taken = train[k, pl.ds(origin * rows + r, examples, stride=dim), :]
@@ -234,37 +296,33 @@
         score(me, k)
 
     late = count - early
-    twice = max(0, min(late, early - 2, count // 2))
-
-    def both(i, carry):
-        forward(early + i)
-        use(2 * i)
-        use(2 * i + 1)
-        return carry
-
-    lax.fori_loop(0, twice, both, 0)
-    lag = early - twice
-    if lag == 0 and late > twice:
-        lag = 2
-        for i in range(lag):
-            forward(early + twice + i)
-        begun = early + twice + lag
-    else:
-        begun = early + twice
-
-    def single(number, carry):
-        forward(number)
-        use(number - lag)
-        return carry
-
-    lax.fori_loop(begun, count, single, 0)
-    done = max(2 * twice, count - lag) if begun < count else 2 * twice
+    each = min(early // late, 3)
+    near_count = (part_size - 1) * slots
+
+    def use_near(number):
+        turn, k = turn_of(number + slots)
+        near_arrival(turn, k).wait_recv()
+        score(near_source(turn), k)
+
+    def late_forward(number, carry):
+        forward(early + number)
+        for at in range(each):
+            use(each * number + at)
+            if each == 3:
+                use_near(each * number + at)
+        return carry
+
+    def near_only(number, carry):
+        use_near(number)
+        return carry
 
     def rest(number, carry):
         use(number)
         return carry
 
-    lax.fori_loop(done, count, rest, 0)
+    lax.fori_loop(0, late, late_forward, 0)
+    lax.fori_loop(late * each if each == 3 else 0, near_count, near_only, 0)
+    lax.fori_loop(each * late, count, rest, 0)
 
     summed = total[...]
     summed = summed[:queries] + summed[queries:]
@@ -289,6 +347,24 @@
     lax.fori_loop(1, n, share_partial, 0)
     parts[0] = part[...]
 
+    def arrived(step, carry):
+        partial(step).wait_recv()
+        return carry
+
+    lax.fori_loop(1, n, arrived, 0)
+
+    def add(owner, running):
+        return running + parts[lax.rem(me + n - owner, n)]
+
+    final = lax.fori_loop(0, n, add, jnp.zeros_like(part))
+    scores_ref[...] = jnp.concatenate([final[:, :examples], final[:, examples:]], axis=0)
+
+    def drained(step, carry):
+        partial(step).wait_send()
+        return carry
+
+    lax.fori_loop(1, n, drained, 0)
+
     def sent(turn, carry):
         for k in range(slots):
             message(turn, k).wait_send()
@@ -296,25 +372,13 @@
                 hand_on(step, turn, k).wait_send()
         return carry
 
-    lax.fori_loop(1, n, sent, 0)
-
-    def arrived(step, carry):
-        partial(step).wait_recv()
-        return carry
-
-    lax.fori_loop(1, n, arrived, 0)
-
-    def add(owner, running):
-        return running + parts[lax.rem(me + n - owner, n)]
-
-    final = lax.fori_loop(0, n, add, jnp.zeros_like(part))
-    scores_ref[...] = jnp.concatenate([final[:, :examples], final[:, examples:]], axis=0)
-
-    def drained(step, carry):
-        partial(step).wait_send()
-        return carry
-
-    lax.fori_loop(1, n, drained, 0)
+    def near_sent(turn, carry):
+        for k in range(slots):
+            near_message(turn, k).wait_send()
+        return carry
+
+    lax.fori_loop(0, part_size, sent, 0)
+    lax.fori_loop(1, part_size, near_sent, 0)
 
 
 def body(n, groups, query_grads, train_grads, out_basis, in_basis, corrections, ranks, slot_modules):
@@ -322,15 +386,22 @@
     slots, examples = train_grads.shape[:2]
     share = queries // groups
     vmem = pl.BlockSpec(memory_space=pltpu.VMEM)
-    smem = pl.BlockSpec(memory_space=pltpu.SMEM)
+    hbm = pl.BlockSpec(memory_space=pltpu.HBM)
     return pl.pallas_call(
         functools.partial(kernel, n, groups),
         out_shape=jax.ShapeDtypeStruct((queries, examples), F32),
-        in_specs=[smem, smem, vmem, pl.BlockSpec(memory_space=pl.ANY), vmem, vmem, vmem],
+        in_specs=[hbm] * 7,
         out_specs=vmem,
         scratch_shapes=[
-            pltpu.VMEM((n, slots, share, rows, dim), F32),
-            pltpu.VMEM((groups, n, slots, share, rows, dim), F32),
+            pltpu.SMEM(slot_modules.shape, jnp.int32),
+            pltpu.SMEM(ranks.shape, jnp.int32),
+            pltpu.VMEM(query_grads.shape, F32),
+            pltpu.VMEM(out_basis.shape, F32),
+            pltpu.VMEM(in_basis.shape, F32),
+            pltpu.VMEM(corrections.shape, F32),
+            pltpu.VMEM((n // 2, slots, share, rows, dim), F32),
+            pltpu.VMEM((n // 2, slots, groups, share, rows, dim), F32),
+            pltpu.VMEM((n, slots, groups, share, rows, dim), F32),
             pltpu.VMEM((slots, examples * dim, dim), F32),
             pltpu.VMEM((slots, 2, 2 * dim, 2 * dim), BF16),
             pltpu.VMEM((slots, 2, 2 * dim, 2 * dim), BF16),
@@ -338,16 +409,19 @@
             pltpu.VMEM((2 * queries, 2 * examples), F32),
             pltpu.VMEM((queries // 2, 2 * examples), F32),
             pltpu.VMEM((n, queries // 2, 2 * examples), F32),
+            pltpu.SemaphoreType.DMA((6,)),
             pltpu.SemaphoreType.DMA((slots,)),
-            pltpu.SemaphoreType.DMA((n, slots)),
-            pltpu.SemaphoreType.DMA((n, slots)),
-            pltpu.SemaphoreType.DMA((groups, n, slots)),
-            pltpu.SemaphoreType.DMA((groups, n, slots)),
+            pltpu.SemaphoreType.DMA((n // 2, slots)),
+            pltpu.SemaphoreType.DMA((n // 2, slots)),
+            pltpu.SemaphoreType.DMA((n // 2, slots)),
+            pltpu.SemaphoreType.DMA((n // 2, slots)),
+            pltpu.SemaphoreType.DMA((groups, n // 2, slots)),
+            pltpu.SemaphoreType.DMA((groups, n // 2, slots)),
             pltpu.SemaphoreType.DMA((n,)),
             pltpu.SemaphoreType.DMA((n,)),
         ],
         compiler_params=pltpu.CompilerParams(
-            collective_id=0, has_side_effects=True, vmem_limit_bytes=48 * 1024 * 1024
+            collective_id=0, has_side_effects=True, vmem_limit_bytes=64 * 1024 * 1024
         ),
     )(
         slot_modules, ranks, query_grads, train_grads.reshape(slots, examples * dim, dim),

time: 86.2 us -> 78.8 us (0.914)
  local copies, waits for them, and re-layouts: 6.22 us -> 1.32 us
  Pallas kernels: 79.7 us -> 77.3 us
    unnamed x13 -> x1, local copies, waits for them, and re-layouts: 6.22 us -> 1.32 us
    pallas_call x1, Pallas kernels: 79.7 us -> 77.3 us  [body(): pl.pallas_call(functools.partial(kernel, n, groups), out_shape=jax.ShapeD...]
where the time goes in v2:
time: 78.8 us; the launch traced here: 78.6 us
  Pallas kernels  77.3 us (98%)
  local copies, waits for them, and re-layouts  1.32 us (2%)
    pallas_call x1, Pallas kernels, body(): pl.pallas_call(functools.partial(kernel, n, groups), out_shape=jax.ShapeD...  77.3 us

profile of v2, /device:TPU:0, one launch (start us, length us, event | category | flops | bytes accessed | tf_op | source)
XLA Modules:
  0.0 78.6 jit_solution(14378056856082454597)
XLA Ops:
  0.0 77.3 %shard_map.73 = f32[32,64]{1,0:T(8,128)} custom-call(s32[32]{0:T(128)} %slots_hbm.1, s32[16]{0:T(128)} %ranks_hbm.1, f32[16,32,8,128]{3,2,1,0:T(8,128)} %query_hbm.1, f32[2,8192,128]{2,1,0:T(8,128)} %bitcast.1, f32[2,128,128]{2,1,0:T(8,128)} %out_basis_hbm.1, f32[2,128,128]{2,1,0:T(8,128)} %in_basis_hbm.1, f32[2,128,128]{2,1,0:T(8,128)} %spectrum_hbm.1), custom_call_target="tpu_custom_call" | custom-call | tf_op jit(solution)/shard_map/pallas_call | solution.py:390
  77.3 1.3 %copy.9 = f32[32,64]{1,0:T(8,128)} copy(f32[32,64]{1,0:T(8,128)} %shard_map.73) | data formatting | bytes 16384

commit v3 on v2

--- a/solution.py
+++ b/solution.py
@@ -139,15 +139,15 @@
             message(turn, k).start()
         return carry
 
-    lax.fori_loop(0, part_size, send, 0)
-
     def send_near(turn, carry):
         for k in range(slots):
             for g in range(groups):
                 direct[turn, k, g] = query_ref[wanted(within(turn), k), pl.ds(g * share, share)]
             near_message(turn, k).start()
-        return carry
-
+            message(turn, k).start()
+        return carry
+
+    send(0, 0)
     lax.fori_loop(1, part_size, send_near, 0)
     for k in range(slots):
         for g in range(groups):

time: 78.8 us -> 69.2 us (0.88)
  Pallas kernels: 77.3 us -> 67.6 us
    pallas_call x1, Pallas kernels: 77.3 us -> 67.6 us  [body(): pl.pallas_call(functools.partial(kernel, n, groups), out_shape=jax.ShapeD...]
where the time goes in v3:
time: 69.2 us; the launch traced here: 69 us
  Pallas kernels  67.6 us (98%)
  local copies, waits for them, and re-layouts  1.32 us (2%)
    pallas_call x1, Pallas kernels, body(): pl.pallas_call(functools.partial(kernel, n, groups), out_shape=jax.ShapeD...  67.6 us

profile of v3, /device:TPU:0, one launch (start us, length us, event | category | flops | bytes accessed | tf_op | source)
XLA Modules:
  0.0 69.0 jit_solution(6530764647732157962)
XLA Ops:
  0.0 67.6 %shard_map.73 = f32[32,64]{1,0:T(8,128)} custom-call(s32[32]{0:T(128)} %slots_hbm.1, s32[16]{0:T(128)} %ranks_hbm.1, f32[16,32,8,128]{3,2,1,0:T(8,128)} %query_hbm.1, f32[2,8192,128]{2,1,0:T(8,128)} %bitcast.1, f32[2,128,128]{2,1,0:T(8,128)} %out_basis_hbm.1, f32[2,128,128]{2,1,0:T(8,128)} %in_basis_hbm.1, f32[2,128,128]{2,1,0:T(8,128)} %spectrum_hbm.1), custom_call_target="tpu_custom_call" | custom-call | tf_op jit(solution)/shard_map/pallas_call | solution.py:390
  67.6 1.3 %copy.9 = f32[32,64]{1,0:T(8,128)} copy(f32[32,64]{1,0:T(8,128)} %shard_map.73) | data formatting | bytes 16384

commit v4 on v3

--- a/solution.py
+++ b/solution.py
@@ -79,32 +79,31 @@
     for step in range(1, groups):
         pl.semaphore_signal(barrier, inc=1, device_id=group_peer(step), device_id_type=MESH)
 
+    mine = me // part_size
+    place = lax.rem(me, part_size)
+
+    def across(turn):
+        return (1 - mine) * part_size + lax.rem(place + turn, part_size)
+
+    def within(turn):
+        return mine * part_size + lax.rem(place + part_size - turn, part_size)
+
+    def source(turn):
+        return (1 - mine) * part_size + lax.rem(place + part_size - turn, part_size)
+
+    def near_source(turn):
+        return mine * part_size + lax.rem(place + turn, part_size)
+
+    def wanted(target, k):
+        return jnp.maximum(slots_ref[target * slots + k], 0)
+
+    loads[0].wait()
+    loads[1].wait()
     load_train = [
         pltpu.make_async_copy(train_ref.at[k], train.at[k], train_sem.at[k]) for k in range(slots)
     ]
     for copy in load_train:
         copy.start()
-
-    mine = me // part_size
-    place = lax.rem(me, part_size)
-
-    def across(turn):
-        return (1 - mine) * part_size + lax.rem(place + turn, part_size)
-
-    def within(turn):
-        return mine * part_size + lax.rem(place + turn, part_size)
-
-    def source(turn):
-        return (1 - mine) * part_size + lax.rem(place + part_size - turn, part_size)
-
-    def near_source(turn):
-        return mine * part_size + lax.rem(place + part_size - turn, part_size)
-
-    def wanted(target, k):
-        return jnp.maximum(slots_ref[target * slots + k], 0)
-
-    loads[0].wait()
-    loads[1].wait()
 
     def fill(turn, carry):
         for k in range(slots):

time: 69.2 us -> 67.8 us (0.980)
  Pallas kernels: 67.6 us -> 66.2 us
    pallas_call x1, Pallas kernels: 67.6 us -> 66.2 us  [body(): pl.pallas_call(functools.partial(kernel, n, groups), out_shape=jax.ShapeD...]
where the time goes in v4:
time: 67.8 us; the launch traced here: 67.5 us
  Pallas kernels  66.2 us (98%)
  local copies, waits for them, and re-layouts  1.32 us (2%)
    pallas_call x1, Pallas kernels, body(): pl.pallas_call(functools.partial(kernel, n, groups), out_shape=jax.ShapeD...  66.2 us

profile of v4, /device:TPU:0, one launch (start us, length us, event | category | flops | bytes accessed | tf_op | source)
XLA Modules:
  0.0 67.5 jit_solution(9632918269174226920)
XLA Ops:
  0.0 66.2 %shard_map.73 = f32[32,64]{1,0:T(8,128)} custom-call(s32[32]{0:T(128)} %slots_hbm.1, s32[16]{0:T(128)} %ranks_hbm.1, f32[16,32,8,128]{3,2,1,0:T(8,128)} %query_hbm.1, f32[2,8192,128]{2,1,0:T(8,128)} %bitcast.1, f32[2,128,128]{2,1,0:T(8,128)} %out_basis_hbm.1, f32[2,128,128]{2,1,0:T(8,128)} %in_basis_hbm.1, f32[2,128,128]{2,1,0:T(8,128)} %spectrum_hbm.1), custom_call_target="tpu_custom_call" | custom-call | tf_op jit(solution)/shard_map/pallas_call | solution.py:389
  66.2 1.3 %copy.9 = f32[32,64]{1,0:T(8,128)} copy(f32[32,64]{1,0:T(8,128)} %shard_map.73) | data formatting | bytes 16384
